TPU v7x, 256 devices: a whole 4x4x8 slice. The times are simulated.
256 devices in a mesh: ctx: 32 (over y, x, core), head: 8 (over z).
Axes of the slice: x: 4, y: 4, z: 8, core: 2. Of those that a mesh axis runs over, the one named last changes fastest.
Arguments:
- q_latent: bfloat16 [4096, 128, 512], P('ctx', 'head'), may hold values from -80 to 80
- q_rope: bfloat16 [4096, 8192], P('ctx', 'head'), may hold values from -80 to 80
- kv_latent: bfloat16 [4096, 16, 512], P('ctx', None, 'head'), may hold values from -6.5 to 6.5
- kv_rope: bfloat16 [4096, 1024], P('ctx'), may hold values from -6.5 to 6.5
- grad_out: bfloat16 [4096, 128, 512], P('ctx', 'head'), may hold values from -6 to 6
- block_slot: int32 [4096], replicated, may hold values from 0 to 4095, as said below
- pool: int32 [32, 32, 2], P('ctx'), may hold values from -1 to 4095, as said below
- selected: int32 [4096, 32], P('ctx'), may hold values from 0 to 63, as said below
Outputs:
- d_q_latent: bfloat16 [4096, 128, 512], P('ctx', 'head')
- d_q_rope: bfloat16 [4096, 8192], P('ctx', 'head')
- d_kv_latent: bfloat16 [4096, 16, 512], P('ctx', None, 'head')
- d_kv_rope: bfloat16 [4096, 1024], P('ctx', 'head')
Inputs may be any that keep to these rules, and one draw needn't show every extreme that they name: `block_slot`: a permutation of the context blocks; storage rows r * 128 to (r + 1) * 128 - 1 belong to ctx index r. pool[s, o] lists distinct blocks owned by ctx index o (block_slot // 128 == o) that queries of shard s select, filled slots first, then -1; no block appears twice in pool[s]; each pool[s, o] has 1 or 2 filled slots, and some owner o has all 2 slots filled in pool[s, o] for every s. selected[t] holds 32 distinct positions of filled slots in pool[t // 128] read as 64 slots in a row.
All inputs are finite; a program needn't handle non-finite values.
Results may differ from a plain program's by a relative error of at most 0.0051.
Values may be sent and summed in bfloat16 or wider, within the bound.
A program may use at most 128 MiB of HBM per device.

v0:
```python
import jax
import jax.numpy as jnp
from jax import lax
from jax.sharding import PartitionSpec as P

SCALE = 192.0 ** (-0.5)


def local(q_latent, q_rope, kv_latent, kv_rope, grad_out, block_slot, pool, selected):
    shards = lax.axis_size("ctx")
    owned = kv_latent.shape[0]
    block_len = kv_latent.shape[1]
    cap = pool.shape[2]
    slots = shards * cap
    queries, heads_here, latent = q_latent.shape
    rope = q_rope.shape[1] // heads_here
    wanted = pool[0]
    filled = wanted >= 0
    table = jnp.arange(block_slot.shape[0], dtype=jnp.int32)
    stored = jnp.sum(
        jnp.where(wanted[:, :, None] == table[None, None, :], block_slot[None, None, :], 0), axis=2
    )
    offset = jnp.arange(shards, dtype=jnp.int32)[:, None] * owned
    local_rows = jnp.where(filled, stored - offset, 0)
    requests = lax.all_to_all(local_rows, "ctx", split_axis=0, concat_axis=0, tiled=True)
    full_latent = lax.all_gather(kv_latent, "head", axis=2, tiled=True)
    pool_latent, pool_rope = (
        lax.all_to_all(full_latent[requests], "ctx", split_axis=0, concat_axis=0, tiled=True),
        lax.all_to_all(kv_rope[requests], "ctx", split_axis=0, concat_axis=0, tiled=True),
    )
    width_keys = slots * block_len
    keys_latent = pool_latent.reshape(width_keys, latent)
    keys_rope = pool_rope.reshape(width_keys, rope)
    q_rot = q_rope.reshape(queries, heads_here, rope)
    chosen = jnp.any(
        selected[:, :, None] == jnp.arange(slots, dtype=jnp.int32)[None, None, :], axis=1
    )
    visible = jnp.repeat(chosen, block_len, axis=1)
    step_rows = 64
    count = queries // step_rows

    def one_block(carry, item):
        acc_latent, acc_rope = carry
        q_lat, q_rt, cotan, seen = item
        scores = jnp.einsum("qhl,kl->qhk", q_lat, keys_latent, preferred_element_type=jnp.float32)
        scores = (
            scores + jnp.einsum("qhr,kr->qhk", q_rt, keys_rope, preferred_element_type=jnp.float32)
        ) * SCALE
        scores = jnp.where(seen[:, None, :], scores, -jnp.inf)
        peak = jnp.max(scores, axis=2, keepdims=True)
        weights = jnp.exp(scores - peak)
        probs = weights / jnp.sum(weights, axis=2, keepdims=True)
        dprobs = jnp.einsum("qhl,kl->qhk", cotan, keys_latent, preferred_element_type=jnp.float32)
        delta = jnp.sum(probs * dprobs, axis=2, keepdims=True)
        dscores = (probs * (dprobs - delta) * SCALE).astype(jnp.bfloat16)
        probs_low = probs.astype(jnp.bfloat16)
        grad_qlat = jnp.einsum(
            "qhk,kl->qhl", dscores, keys_latent, preferred_element_type=jnp.float32
        ).astype(jnp.bfloat16)
        grad_qrot = jnp.einsum(
            "qhk,kr->qhr", dscores, keys_rope, preferred_element_type=jnp.float32
        ).astype(jnp.bfloat16)
        acc_latent = acc_latent + jnp.einsum(
            "qhk,qhl->kl", dscores, q_lat, preferred_element_type=jnp.float32
        )
        acc_latent = acc_latent + jnp.einsum(
            "qhk,qhl->kl", probs_low, cotan, preferred_element_type=jnp.float32
        )
        acc_rope = acc_rope + jnp.einsum(
            "qhk,qhr->kr", dscores, q_rt, preferred_element_type=jnp.float32
        )
        return ((acc_latent, acc_rope), (grad_qlat, grad_qrot))

    start = (
        jnp.zeros((width_keys, latent), jnp.float32),
        jnp.zeros((width_keys, rope), jnp.float32),
    )
    items = (
        q_latent.reshape(count, step_rows, heads_here, latent),
        q_rot.reshape(count, step_rows, heads_here, rope),
        grad_out.reshape(count, step_rows, heads_here, latent),
        visible.reshape(count, step_rows, width_keys),
    )
    (grad_latent, grad_rope), (part_qlat, part_qrot) = lax.scan(one_block, start, items)
    d_q_latent = part_qlat.reshape(queries, heads_here, latent)
    d_q_rope = part_qrot.reshape(queries, heads_here * rope)
    grad_latent = grad_latent.reshape(shards, cap, block_len, latent)
    grad_rope = grad_rope.reshape(shards, cap, block_len * rope)
    flat_requests = requests.reshape(slots)
    got_latent, got_rope = (
        lax.all_to_all(grad_latent, "ctx", split_axis=0, concat_axis=0, tiled=True),
        lax.all_to_all(grad_rope, "ctx", split_axis=0, concat_axis=0, tiled=True),
    )
    width = got_latent.shape[3]
    summed_latent = (
        jnp.zeros((owned, block_len, width), jnp.float32)
        .at[flat_requests]
        .add(got_latent.reshape(slots, block_len, width))
    )
    summed_rope = (
        jnp.zeros((owned, got_rope.shape[2]), jnp.float32)
        .at[flat_requests]
        .add(got_rope.reshape(slots, got_rope.shape[2]))
    )
    out_latent, out_rope = (
        lax.psum_scatter(summed_latent, "head", scatter_dimension=2, tiled=True),
        lax.psum_scatter(summed_rope, "head", scatter_dimension=1, tiled=True),
    )
    return (d_q_latent, d_q_rope, out_latent.astype(jnp.bfloat16), out_rope.astype(jnp.bfloat16))


def solution(mesh):
    return jax.shard_map(
        local,
        mesh=mesh,
        in_specs=(
            P("ctx", "head", None),
            P("ctx", "head"),
            P("ctx", None, "head"),
            P("ctx", None),
            P("ctx", "head", None),
            P(),
            P("ctx", None, None),
            P("ctx", None),
        ),
        out_specs=(
            P("ctx", "head", None),
            P("ctx", "head"),
            P("ctx", None, "head"),
            P("ctx", "head"),
        ),
        check_vma=False,
    )
```

profile of v0, /device:TPU:1, one launch (start us, length us, event | category | flops | bytes accessed | tf_op | source)
XLA Modules:
  0.0 346.8 jit_solution(17000684935951401226)
XLA Ops:
  7.2 1.9 copy.51
  9.1 1.0 select_reduce_fusion
  10.2 0.7 bitcast_select_fusion
  10.8 0.1 copy.52
  10.9 15.3 %all_to_all.29 = s32[32,1,2]{2,1,0:T(1,128)S(1)} all-to-all(s32[32,1,2]{2,1,0:T(1,128)S(1)} %copy.52), channel_id=1, replica_groups=mesh['ctx'=32,'head'=8] {'ctx'}, dimensions={0} | all-to-all | bytes 512 | tf_op jit(solution)/shard_map/all_to_all | solution.py:25
  26.2 0.1 copy.53
  26.3 0.1 copy.54
  26.4 0.1 reshape.166
  26.5 0.3 copy-done.6
  26.9 0.7 gather_fusion.1
  27.6 0.7 reshape.173
  28.3 4.2 %all-to-all-start.2 = ((bf16[32,2,1024]{2,1,0:T(2,128)(2,1)}), bf16[32,2,1024]{2,1,0:T(2,128)(2,1)S(1)}, u32[]{:S(2)}, u32[]{:S(2)}) async-start(bf16[32,2,1024]{2,1,0:T(2,128)(2,1)} %reshape.173), calls=%async_computation.2 | async-start | bytes 262144 | tf_op jit(solution)/shard_map/all_to_all | solution.py:29
  32.5 19.2 %all-gather.2.cloned.1.call-done = bf16[128,16,512]{0,1,2:T(8,128)(2,1)} async-done(((bf16[128,16,64]{0,1,2:T(8,128)(2,1)}), bf16[128,16,512]{0,1,2:T(8,128)(2,1)}) %all-gather.2.cloned.1.call-update) | async-done | bytes 2097168 | tf_op jit(solution)/shard_map/all_gather | solution.py:26
  51.6 4.8 %copy.55 = bf16[128,16,512]{2,1,0:T(8,128)(2,1)} copy(bf16[128,16,512]{0,1,2:T(8,128)(2,1)} %all-gather.2.cloned.1.call-done) | data formatting | bytes 4194304 | tf_op jit(solution)/shard_map/all_gather | solution.py:26
  56.4 3.3 gather_fusion
  59.8 11.2 %all-to-all-start.1 = ((bf16[32,2,16,512]{3,2,1,0:T(8,128)(2,1)}), bf16[32,2,16,512]{3,2,1,0:T(8,128)(2,1)S(1)}, u32[]{:S(2)}, u32[]{:S(2)}) async-start(bf16[32,2,16,512]{3,2,1,0:T(8,128)(2,1)} %bitcast.115), calls=%async_computation.1 | async-start | bytes 2097152 | tf_op jit(solution)/shard_map/all_to_all | solution.py:28
  71.1 0.1 fusion.53
  71.2 0.7 broadcast_in_dim.74
  71.9 2.7 reshape_reshape.6
  74.6 2.0 copy.56
  76.6 2.2 reshape_reshape.7
  78.8 0.9 reshape.155
  79.7 1.1 copy.57
  80.7 7.5 %all-to-all-done.1 = bf16[32,2,16,512]{3,2,1,0:T(8,128)(2,1)S(1)} async-done(((bf16[32,2,16,512]{3,2,1,0:T(8,128)(2,1)}), bf16[32,2,16,512]{3,2,1,0:T(8,128)(2,1)S(1)}, u32[]{:S(2)}, u32[]{:S(2)}) %all-to-all-start.1) | async-done | bytes 1048608 | tf_op jit(solution)/shard_map/all_to_all | solution.py:28
  88.2 135.3 %while.17 = (s32[]{:T(128)}, f32[1024,512]{1,0:T(8,128)}, f32[1024,64]{0,1:T(8,128)}, bf16[2,64,16,512]{3,2,1,0:T(8,128)(2,1)}, bf16[2,64,16,64]{3,2,1,0:T(8,128...) while((s32[]{:T(128)}, f32[1024,512]{1,0:T(8,128)}, ...), condition=%wide.region_6.7_spmd.clone, body=%wide.region_2.6_spmd.clone.sunk | while | flops 5811416064 | bytes 145199344 | solution.py:84
  88.2 1.8 fusion.103
  90.0 1.4 multiply_select_fusion.2
  91.5 3.8 %fusion.104 = (f32[64,16]{1,0:T(8,128)}, f32[64,16,1024]{2,1,0:T(8,128)}) fusion(f32[64,16,1024]{2,1,0:T(8,128)S(1)} %multiply_select_fusion.2), kind=kOutput, calls=%fused_computation.71.clone.1 | output fusion | flops 2098175 | bytes 8392704 | tf_op jit(solution)/shard_map/while/body/eval_jaxpr/sub | solution.py:51
  95.3 7.3 %fusion.105 = f32[1024,512,1]{1,0,2:T(8,128)} fusion(bf16[2,64,16,512]{3,2,1,0:T(8,128)(2,1)S(1)} %get-tuple-element.280, s32[]{:T(128)S(6)} %copy.68, f32[64,16]{1,0:T(8,128)} %get-tuple-element.242, f32[64,16,1024]{2,1,0:T(8,128)} %copy-done.1), kind=kOutput, calls=%fused_computation.13.clone.1 | convolution fusion | flops 1076889600 | bytes 11567108 | tf_op jit(solution)/shard_map/while/body/eval_jaxpr/qhk,qhl->kl/dot_general | solution.py:66
  102.6 3.3 fusion.106
  105.8 14.2 %bitcast_add_fusion.3 = f32[1024,512]{1,0:T(8,128)} fusion(f32[1024,512,1]{1,0,2:T(8,128)} %fusion.105, f32[1024,512]{1,0:T(8,128)} %get-tuple-element.258, pred[]{:T(512)S(6)} %compare.3, bf16[2,64,16,512]{3,2,1,0:T(8,128)(2,1)} %get-tuple-element.276, s32[]{:T(128)S(6)} %copy.68, f32[64,16,1024]{2,1,0:T(8,128)} %fusion.106, ...), kind=kOutput, calls=%fused_computation.11.clone.1 | convolution fusion | flops 1082656768 | bytes 24182788 | tf_op jit(solution)/shard_map/while/body/eval_jaxpr/qhk,qhl->kl/dot_general | solution.py:63
  120.0 12.3 %fusion.107 = f32[1024,64]{0,1:T(8,128)} fusion(f32[64,16,1024]{2,1,0:T(8,128)} %fusion.106, f32[1024,64]{0,1:T(8,128)} %get-tuple-element.259, bf16[2,64,16,64]{3,2,1,0:T(8,128)(2,1)} %get-tuple-element.278, s32[]{:T(128)S(6)} %copy.68, pred[]{:T(512)S(6)} %compare.3, f32[64,16,1024]{2,1,0:T(8,128)} %get-tuple-element.243, ...), kind=kOutput, calls=%fused_computation.21.clone.1 | convolution fusion | flops 141690880 | bytes 17629188 | tf_op jit(solution)/shard_map/while/body/eval_jaxpr/qhk,qhr->kr/dot_general | solution.py:69
  132.3 11.3 %fusion.108 = bf16[2,64,16,512]{3,2,1,0:T(8,128)(2,1)} fusion(bf16[2,64,16,512]{3,2,1,0:T(8,128)(2,1)} %get-tuple-element.260, s32[]{:T(128)S(6)} %copy.68, bf16[1024,512]{1,0:T(8,128)(2,1)S(1)} %get-tuple-element.277, f32[64,16,1024]{2,1,0:T(8,128)} %fusion.106, f32[64,16,1024]{2,1,0:T(8,128)} %get-tuple-element.243, f32[64,16]{1,0:T(8,128)} %get-tuple-element.242), kind=kOutput, calls=%fused_computation.18.clone.1 | convolution fusion | flops 1081608192 | bytes 18939908 | tf_op jit(solution)/shard_map/while/body/eval_jaxpr/qhk,kl->qhl/dot_general | solution.py:57
  143.7 11.9 %fusion.109 = bf16[2,64,16,64]{3,2,1,0:T(8,128)(2,1)} fusion(bf16[2,64,16,64]{3,2,1,0:T(8,128)(2,1)} %get-tuple-element.261, s32[]{:T(128)S(6)} %copy.68, f32[64,16,1024]{2,1,0:T(8,128)} %fusion.106, bf16[1024,64]{0,1:T(8,128)(2,1)S(1)} %get-tuple-element.279, f32[64,16,1024]{2,1,0:T(8,128)} %get-tuple-element.243, f32[64,16]{1,0:T(8,128)} %get-tuple-element.242), kind=kOutput, calls=%fused_computation.23.clone.1 | convolution fusion | flops 141625344 | bytes 17235972 | tf_op jit(solution)/shard_map/while/body/eval_jaxpr/qhk,kr->qhr/dot_general | solution.py:60
  155.6 1.8 fusion.103
  157.4 1.4 multiply_select_fusion.2
  158.8 3.8 %fusion.104 = (f32[64,16]{1,0:T(8,128)}, f32[64,16,1024]{2,1,0:T(8,128)}) fusion(f32[64,16,1024]{2,1,0:T(8,128)S(1)} %multiply_select_fusion.2), kind=kOutput, calls=%fused_computation.71.clone.1 | output fusion | flops 2098175 | bytes 8392704 | tf_op jit(solution)/shard_map/while/body/eval_jaxpr/sub | solution.py:51
  162.6 7.3 %fusion.105 = f32[1024,512,1]{1,0,2:T(8,128)} fusion(bf16[2,64,16,512]{3,2,1,0:T(8,128)(2,1)S(1)} %get-tuple-element.280, s32[]{:T(128)S(6)} %copy.68, f32[64,16]{1,0:T(8,128)} %get-tuple-element.242, f32[64,16,1024]{2,1,0:T(8,128)} %copy-done.1), kind=kOutput, calls=%fused_computation.13.clone.1 | convolution fusion | flops 1076889600 | bytes 11567108 | tf_op jit(solution)/shard_map/while/body/eval_jaxpr/qhk,qhl->kl/dot_general | solution.py:66
  169.9 3.3 fusion.106
  173.2 14.8 %bitcast_add_fusion.3 = f32[1024,512]{1,0:T(8,128)} fusion(f32[1024,512,1]{1,0,2:T(8,128)} %fusion.105, f32[1024,512]{1,0:T(8,128)} %get-tuple-element.258, pred[]{:T(512)S(6)} %compare.3, bf16[2,64,16,512]{3,2,1,0:T(8,128)(2,1)} %get-tuple-element.276, s32[]{:T(128)S(6)} %copy.68, f32[64,16,1024]{2,1,0:T(8,128)} %fusion.106, ...), kind=kOutput, calls=%fused_computation.11.clone.1 | convolution fusion | flops 1082656768 | bytes 24182788 | tf_op jit(solution)/shard_map/while/body/eval_jaxpr/qhk,qhl->kl/dot_general | solution.py:63
  187.9 12.3 %fusion.107 = f32[1024,64]{0,1:T(8,128)} fusion(f32[64,16,1024]{2,1,0:T(8,128)} %fusion.106, f32[1024,64]{0,1:T(8,128)} %get-tuple-element.259, bf16[2,64,16,64]{3,2,1,0:T(8,128)(2,1)} %get-tuple-element.278, s32[]{:T(128)S(6)} %copy.68, pred[]{:T(512)S(6)} %compare.3, f32[64,16,1024]{2,1,0:T(8,128)} %get-tuple-element.243, ...), kind=kOutput, calls=%fused_computation.21.clone.1 | convolution fusion | flops 141690880 | bytes 17629188 | tf_op jit(solution)/shard_map/while/body/eval_jaxpr/qhk,qhr->kr/dot_general | solution.py:69
  200.3 11.3 %fusion.108 = bf16[2,64,16,512]{3,2,1,0:T(8,128)(2,1)} fusion(bf16[2,64,16,512]{3,2,1,0:T(8,128)(2,1)} %get-tuple-element.260, s32[]{:T(128)S(6)} %copy.68, bf16[1024,512]{1,0:T(8,128)(2,1)S(1)} %get-tuple-element.277, f32[64,16,1024]{2,1,0:T(8,128)} %fusion.106, f32[64,16,1024]{2,1,0:T(8,128)} %get-tuple-element.243, f32[64,16]{1,0:T(8,128)} %get-tuple-element.242), kind=kOutput, calls=%fused_computation.18.clone.1 | convolution fusion | flops 1081608192 | bytes 18939908 | tf_op jit(solution)/shard_map/while/body/eval_jaxpr/qhk,kl->qhl/dot_general | solution.py:57
  211.6 11.9 %fusion.109 = bf16[2,64,16,64]{3,2,1,0:T(8,128)(2,1)} fusion(bf16[2,64,16,64]{3,2,1,0:T(8,128)(2,1)} %get-tuple-element.261, s32[]{:T(128)S(6)} %copy.68, f32[64,16,1024]{2,1,0:T(8,128)} %fusion.106, bf16[1024,64]{0,1:T(8,128)(2,1)S(1)} %get-tuple-element.279, f32[64,16,1024]{2,1,0:T(8,128)} %get-tuple-element.243, f32[64,16]{1,0:T(8,128)} %get-tuple-element.242), kind=kOutput, calls=%fused_computation.23.clone.1 | convolution fusion | flops 141625344 | bytes 17235972 | tf_op jit(solution)/shard_map/while/body/eval_jaxpr/qhk,kr->qhr/dot_general | solution.py:60
  223.5 1.2 copy.59
  224.6 0.3 reshape.162
  224.9 12.4 %all_to_all.30 = f32[32,2,1024]{2,1,0:T(2,128)S(1)} all-to-all(f32[32,2,1024]{2,1,0:T(2,128)S(1)} %reshape.162), channel_id=1, replica_groups=mesh['ctx'=32,'head'=8] {'ctx'}, dimensions={0} | all-to-all | bytes 524288 | tf_op jit(solution)/shard_map/all_to_all | solution.py:92
  237.3 3.9 %all-to-all-start.3 = ((f32[32,2,16,512]{3,2,1,0:T(8,128)}), f32[32,2,16,512]{3,2,1,0:T(8,128)S(1)}, u32[]{:S(2)}, u32[]{:S(2)}) async-start(f32[32,2,16,512]{3,2,1,0:T(8,128)} %bitcast.116), calls=%async_computation.3 | async-start | bytes 4194304 | tf_op jit(solution)/shard_map/all_to_all | solution.py:91
  241.2 0.0 reduce-scatter.5.cloned.1.call-start
  241.3 0.5 broadcast.133
  241.8 0.7 reduce.3
  242.5 0.1 reshape.159
  242.6 0.2 reshape.192
  242.8 1.9 scatter_custom_fusion.1
  244.7 0.0 reduce-scatter.3.cloned.1.call-start
  244.8 24.4 %all-to-all-done.3 = f32[32,2,16,512]{3,2,1,0:T(8,128)S(1)} async-done(((f32[32,2,16,512]{3,2,1,0:T(8,128)}), f32[32,2,16,512]{3,2,1,0:T(8,128)S(1)}, u32[]{:S(2)}, u32[]{:S(2)}) %all-to-all-start.3) | async-done | bytes 2097184 | tf_op jit(solution)/shard_map/all_to_all | solution.py:91
  269.2 2.5 broadcast_in_dim.77
  271.7 9.1 %scatter_fusion = f32[128,16,512]{2,1,0:T(8,128)} fusion(f32[128,16,512]{2,1,0:T(8,128)} %broadcast_in_dim.77, s32[64]{0:T(128)S(1)} %fusion.56, f32[64,16,512]{2,1,0:T(8,128)S(1)} %bitcast.114), kind=kCustom, calls=%fused_computation.2 | custom fusion | flops 524288 | bytes 6291712 | tf_op jit(solution)/shard_map/scatter-add | solution.py:98
  280.8 5.8 %copy.58 = f32[128,16,512]{0,1,2:T(8,128)} copy(f32[128,16,512]{2,1,0:T(8,128)} %scatter_fusion) | data formatting | bytes 8388608 | tf_op jit(solution)/shard_map/scatter-add | solution.py:98
  286.6 1.0 copy-done.5
  287.6 1.1 reshape.158
  288.7 1.5 convert_element_type.19
  290.1 48.3 %reduce-scatter.3.cloned.1.call-done = f32[128,16,64]{0,1,2:T(8,128)} async-done(((f32[128,16,512]{0,1,2:T(8,128)}), f32[128,16,64]{0,1,2:T(8,128)}) %reduce-scatter.3.cloned.1.call-update) | async-done | bytes 524304 | tf_op jit(solution)/shard_map/reduce_scatter | solution.py:106
  338.4 1.1 convert_element_type.18
  339.5 0.8 copy.60
  (38 shorter events, 0.2 us)
Async XLA Ops:
  7.2 19.7 %copy-start = (bf16[128,1024]{1,0:T(8,128)(2,1)S(1)}, bf16[128,1024]{1,0:T(8,128)(2,1)}, u32[]{:S(2)}) copy-start(bf16[128,1024]{1,0:T(8,128)(2,1)} %param.13) | copy-start | bytes 786436
  7.2 44.4 %all-gather.2.cloned.1.call-start = ((), (), s32[]{:S(2)}) async-start(), calls=%async_computation.7 | async-start | bytes 2359296 | tf_op jit(solution)/shard_map/all_gather | solution.py:26
  26.2 0.6 copy-start.6
  28.3 31.5 %all-to-all-start.2 = ((bf16[32,2,1024]{2,1,0:T(2,128)(2,1)}), bf16[32,2,1024]{2,1,0:T(2,128)(2,1)S(1)}, u32[]{:S(2)}, u32[]{:S(2)}) async-start(bf16[32,2,1024]{2,1,0:T(2,128)(2,1)} %reshape.173), calls=%async_computation.2 | async-start | bytes 262144 | tf_op jit(solution)/shard_map/all_to_all | solution.py:29
  32.4 38.6 %copy-start.8 = (s32[128,32]{0,1:T(8,128)S(1)}, s32[128,32]{0,1:T(8,128)}, u32[]{:S(2)}) copy-start(s32[128,32]{0,1:T(8,128)} %param.17) | copy-start | bytes 49156
  56.4 31.8 %copy-start.2 = (bf16[128,16,512]{2,1,0:T(8,128)(2,1)S(1)}, bf16[128,16,512]{2,1,0:T(8,128)(2,1)}, u32[]{:S(2)}) copy-start(bf16[128,16,512]{2,1,0:T(8,128)(2,1)} %param.14) | copy-start | bytes 6291460
  59.8 28.4 %all-to-all-start.1 = ((bf16[32,2,16,512]{3,2,1,0:T(8,128)(2,1)}), bf16[32,2,16,512]{3,2,1,0:T(8,128)(2,1)S(1)}, u32[]{:S(2)}, u32[]{:S(2)}) async-start(bf16[32,2,16,512]{3,2,1,0:T(8,128)(2,1)} %bitcast.115), calls=%async_computation.1 | async-start | bytes 2097152 | tf_op jit(solution)/shard_map/all_to_all | solution.py:28
  88.2 1.8 copy-start.4
  88.2 1.8 copy-start.3
  91.5 3.8 %copy-start.1 = (f32[64,16,1024]{2,1,0:T(8,128)}, f32[64,16,1024]{2,1,0:T(8,128)S(1)}, u32[]{:S(2)}) copy-start(f32[64,16,1024]{2,1,0:T(8,128)S(1)} %multiply_select_fusion.2) | copy-start | bytes 12582916 | tf_op jit(solution)/shard_map/while
  155.5 1.8 copy-start.4
  155.6 1.8 copy-start.3
  158.8 3.8 %copy-start.1 = (f32[64,16,1024]{2,1,0:T(8,128)}, f32[64,16,1024]{2,1,0:T(8,128)S(1)}, u32[]{:S(2)}) copy-start(f32[64,16,1024]{2,1,0:T(8,128)S(1)} %multiply_select_fusion.2) | copy-start | bytes 12582916 | tf_op jit(solution)/shard_map/while
  223.5 18.3 %copy-start.7 = (s32[32,1,2]{2,1,0:T(1,128)S(1)}, s32[32,1,2]{2,1,0:T(1,128)}, u32[]{:S(2)}) copy-start(s32[32,1,2]{2,1,0:T(1,128)} %copy-done.6) | copy-start | bytes 772
  237.3 31.9 %all-to-all-start.3 = ((f32[32,2,16,512]{3,2,1,0:T(8,128)}), f32[32,2,16,512]{3,2,1,0:T(8,128)S(1)}, u32[]{:S(2)}, u32[]{:S(2)}) async-start(f32[32,2,16,512]{3,2,1,0:T(8,128)} %bitcast.116), calls=%async_computation.3 | async-start | bytes 4194304 | tf_op jit(solution)/shard_map/all_to_all | solution.py:91
  241.2 47.4 %reduce-scatter.5.cloned.1.call-start = ((), (), s32[]{:S(2)}) async-start(), calls=%async_computation.9 | async-start | bytes 589824 | tf_op jit(solution)/shard_map/reduce_scatter | solution.py:107
  244.7 93.7 %reduce-scatter.3.cloned.1.call-start = ((), (), s32[]{:S(2)}) async-start(), calls=%async_computation.8 | async-start | bytes 4718592 | tf_op jit(solution)/shard_map/reduce_scatter | solution.py:106
  286.6 1.0 copy-start.5
Sparse Core Ops, SparseCore 0:
  10.4 41.1 all-gather.1
  244.9 31.8 reduce-scatter.4
  286.7 51.6 reduce-scatter.2
where the time goes:
time: 348 us; the launch traced here: 347 us
  matrix products  128 us (37%)
  waiting for transfers between devices  99.3 us (29%)
  local copies, waits for them, and re-layouts  35.1 us (10%)
  blocking collectives  27.7 us (8%)
  other arithmetic  23.6 us (7%)
  starting transfers between devices  19.4 us (6%)
  between operations  13.9 us (4%)
    reduce_scatter x1, waiting for transfers between devices, local(): lax.psum_scatter(summed_latent, 'head', scatter_dimension=2, tiled=True)  48.3 us
    dot_general x2, matrix products, one_block(): jnp.einsum('qhk,qhl->kl', dscores, q_lat, preferred_element_type=jnp.floa...  28.9 us
    dot_general x2, matrix products, one_block(): jnp.einsum('qhk,qhr->kr', dscores, q_rt, preferred_element_type=jnp.float32)  24.7 us
    all_to_all x1, waiting for transfers between devices, local(): lax.all_to_all(grad_latent, 'ctx', split_axis=0, concat_axis=0, tiled=True)  24.4 us
    dot_general x2, matrix products, one_block(): jnp.einsum('qhk,kr->qhr', dscores, keys_rope, preferred_element_type=jnp....  23.7 us
    dot_general x2, matrix products, one_block(): jnp.einsum('qhk,kl->qhl', dscores, keys_latent, preferred_element_type=jn...  22.7 us
    all_gather x1, waiting for transfers between devices, local(): full_latent = lax.all_gather(kv_latent, 'head', axis=2, tiled=True)  19.2 us
    all_to_all x1, blocking collectives, local(): lax.all_to_all(local_rows, 'ctx', split_axis=0, concat_axis=0, tiled=True)  15.3 us
  transfers between devices with their start and end apart: 6, of which 4 were waited for; matrix products, arithmetic and copies ran while one was open for 13% of the time, Pallas kernels for 0%

commit v1 on v0

v1 whole, which is shorter than its diff:
```python
import functools

import jax
import jax.numpy as jnp
from jax import lax
from jax.experimental import pallas as pl
from jax.experimental.pallas import tpu as pltpu
from jax.sharding import PartitionSpec as P

SCALE = 192.0 ** (-0.5)
LOG2E = 1.4426950408889634
BIG = 1e30
MESH = pl.DeviceIdType.MESH
F32 = jnp.float32
BF16 = jnp.bfloat16
TOK = 16
HALF = 64
LANES = 128
NT_MAX = 4
PIECE, DELAY, ARRIVE = 0.85, 1.5, 1.0
T_SCORE, T_GRAD, T_DQ, T_EVENT = 0.9, 0.75, 0.55, 0.1


def hops_of(nr, t, d):
    return nr if (t + d) % 2 == 0 else nr - 1


def plan(nt, nr, steps, opens, needs):
    order, free, now, left = [], [0.0, 0.0], 0.0, {t: 2 for t in range(nt)}
    ready = [(at, t, d, 1) for t, at in opens.items() if not isinstance(at, tuple) for d in range(2)]
    whole = {}
    steps = list(steps)
    while steps or ready:
        due = [e for e in ready if e[0] <= now]
        if due:
            event = min(due)
            ready.remove(event)
            _, t, d, r = event
            order.append(("event", t, d, r))
            now += T_EVENT
            if r <= hops_of(nr, t, d):
                free[d] = max(now, free[d]) + PIECE
                ready.append((free[d] + DELAY, t, d, r + 1))
            else:
                left[t] -= 1
                if left[t] == 0:
                    order.append(("whole", t))
                    whole[t] = now
            continue
        if steps and (not needs or steps[0][2] in whole):
            name, took, _ = steps.pop(0)
            order.append(("step",) + name)
            now += took
            for t, at in opens.items():
                if at == name:
                    ready += [(now, t, d, 1) for d in range(2)]
            continue
        now = min(e[0] for e in ready)
    return order


def dot(a, b, ca=1, cb=0):
    return lax.dot_general(a, b, (((ca,), (cb,)), ((), ())), preferred_element_type=F32)


def iota(shape, dim):
    return lax.broadcasted_iota(jnp.int32, shape, dim)


def cat(*parts):
    return jnp.concatenate(parts, axis=1)


def kernel(
    ns, nz, nt, nrb, rb,
    pool_ref, slot_ref, sel_ref, qrope_ref, kvl_ref, kvr_ref, q_hbm, do_hbm,
    dq_hbm, dqr_out, yin, gsc,
    req, reqs, qx, xf, xs, xin, kall, kaug, qaug, qdo, ebuf, dpbuf, stat, fin, dst, acc,
    prs, pf, rs_out, rs_in, yf, ys, dqst,
    req_sem, x_sem, y_sem, send_sem, ag_s, ag_r, rs_s, rs_r, in_sem, out_sem,
):
    s = lax.axis_index("ctx")
    z = lax.axis_index("head")
    jc = ns // nt
    kh = jc * TOK
    kc = 2 * kh
    nr = nz // 2
    ii_n = TOK // nz
    latent = nz * HALF
    owned = kvl_ref.shape[1]
    qd = sel_ref.shape[1]
    heads = (nrb * rb) // qd
    right = lax.rem(z + 1, nz)
    left = lax.rem(z + nz - 1, nz)

    def hops(t, d):
        return hops_of(nr, t, d)

    barrier = pltpu.get_barrier_semaphore()

    @pl.loop(1, ns)
    def _(j):
        pl.semaphore_signal(barrier, inc=1, device_id=(lax.rem(s + j, ns), z), device_id_type=MESH)

    for zn in (left, right):
        pl.semaphore_signal(barrier, inc=1, device_id=(s, zn), device_id_type=MESH)

    in_copies = [
        pltpu.make_async_copy(q_hbm, qaug.at[:, :, pl.ds(0, latent)], in_sem.at[0]),
        pltpu.make_async_copy(do_hbm, qdo.at[:, pl.ds(rb, rb)], in_sem.at[1]),
        pltpu.make_async_copy(q_hbm, qdo.at[:, pl.ds(0, rb)], in_sem.at[2]),
    ]
    for copy in in_copies:
        copy.start()

    pools = pool_ref[...].astype(F32)
    wanted = cat(pools[0:1], pools[1:2], jnp.full((1, LANES - 2 * ns), -1.0, F32))
    wanted = jnp.broadcast_to(wanted, (LANES, LANES))
    eye = iota((LANES, LANES), 0) == iota((LANES, LANES), 1)
    lane = iota((LANES, LANES), 1)
    col = jnp.sum(jnp.where(eye, wanted, 0.0), axis=1, keepdims=True)
    coli = col.astype(jnp.int32)
    hi = jnp.right_shift(coli, 7)
    lo = jnp.bitwise_and(coli, 127)
    nhi = slot_ref.shape[0]
    onehot = (iota((LANES, nhi), 1) == hi).astype(F32).astype(BF16)
    table = slot_ref[...]
    t_hi = jnp.right_shift(table, 6).astype(F32).astype(BF16)
    t_lo = jnp.bitwise_and(table, 63).astype(F32).astype(BF16)
    rows = dot(onehot, t_hi) * 64.0 + dot(onehot, t_lo)
    rowcol = jnp.sum(jnp.where(lane == lo, rows, 0.0), axis=1, keepdims=True)
    rowcol = jnp.where(col >= 0.0, rowcol, -1.0)
    reqs[...] = jnp.sum(
        jnp.where(eye, jnp.broadcast_to(rowcol, (LANES, LANES)), 0.0), axis=0, keepdims=True
    )
    req[0] = reqs[...]

    pl.semaphore_wait(barrier, ns + 1)

    @pl.loop(1, ns)
    def _(j):
        pltpu.make_async_remote_copy(
            src_ref=reqs, dst_ref=req.at[j], send_sem=send_sem.at[0], recv_sem=req_sem,
            device_id=(lax.rem(s + ns - j, ns), z), device_id_type=MESH,
        ).start()

    yf[...] = jnp.zeros_like(yf)
    places = iota((HALF, 1), 0)
    cpos = places // ns
    slotv = 2 * lax.rem(s + 2 * ns - (places - cpos * ns), ns) + cpos
    slotv = jnp.where(places < 2 * ns, slotv, -5)
    sel = sel_ref[...]
    absent = jnp.ones((HALF, qd), F32)
    for k in range(sel.shape[0]):
        absent = jnp.where(sel[k : k + 1, :] == slotv, 0.0, absent)
    unit = (iota((HALF, HALF), 0) == iota((HALF, HALF), 1)).astype(F32).astype(BF16)
    missing = dot(absent.astype(BF16), unit, 0, 0)
    for h in range(heads):
        rope_h = qrope_ref[:, h * HALF : (h + 1) * HALF].astype(F32)
        qx[pl.ds(h, qd, stride=heads), :] = cat(rope_h, missing)
    qaug[:, :, latent : latent + LANES] = qx[...].astype(BF16).reshape(nrb, rb, LANES)

    pltpu.make_async_copy(req.at[pl.ds(1, ns - 1)], req.at[pl.ds(1, ns - 1)], req_sem).wait()
    got = req[...].reshape(ns, LANES)
    lane_s = iota((ns, LANES), 1)
    base = (owned * s).astype(F32)
    picks = []
    for c in range(2):
        mine = jnp.sum(jnp.where(lane_s == c * ns + s, got, 0.0), axis=1, keepdims=True) - base
        picks.append((iota((ns, owned), 1).astype(F32) == mine).astype(F32))
    gsc[...] = jnp.concatenate(picks, axis=0).astype(BF16)
    g = gsc[...]
    lat = dot(g, kvl_ref[...], 1, 1)
    rop = dot(g, kvr_ref[...])
    for i in range(TOK):
        sl = slice(i * HALF, (i + 1) * HALF)
        xf[pl.ds(i, ns, stride=2 * TOK), :] = cat(lat[:ns, sl], lat[ns:, sl])
        xf[pl.ds(TOK + i, ns, stride=2 * TOK), :] = cat(rop[:ns, sl], rop[ns:, sl])
    xs[...] = xf[...].astype(BF16).reshape(xs.shape)
    xin[0] = xs[0]

    @pl.loop(1, ns)
    def _(j):
        pltpu.make_async_remote_copy(
            src_ref=xs.at[j], dst_ref=xin.at[j], send_sem=send_sem.at[1], recv_sem=x_sem.at[j // jc],
            device_id=(lax.rem(s + j, ns), z), device_id_type=MESH,
        ).start()

    def chunk(t):
        return pl.ds(t * jc, jc)

    def ag_copy(t, d, r):
        zs = lax.rem(z + nz - (r - 1), nz) if d == 0 else lax.rem(z + (r - 1), nz)
        piece = kall.at[zs, chunk(t)]
        return pltpu.make_async_remote_copy(
            src_ref=piece, dst_ref=piece, send_sem=ag_s.at[t, d, r - 1], recv_sem=ag_r.at[t, d, r - 1],
            device_id=(s, right if d == 0 else left), device_id_type=MESH,
        )

    def ag_wait(t, d, r):
        zs = lax.rem(z + nz - r, nz) if d == 0 else lax.rem(z + r, nz)
        piece = kall.at[zs, chunk(t)]
        pltpu.make_async_copy(piece, piece, ag_r.at[t, d, r - 1]).wait()

    def ag_event(t, d, r):
        if r == 1 and d == 0:
            first = 1 if t == 0 else t * jc
            part = xin.at[pl.ds(first, (t + 1) * jc - first)]
            pltpu.make_async_copy(part, part, x_sem.at[t]).wait()
            kall[z, chunk(t)] = xin[chunk(t), :TOK, :]
        if r > 1:
            ag_wait(t, d, r - 1)
        if r <= hops(t, d):
            ag_copy(t, d, r).start()

    lane_k = iota((kh, LANES), 1)
    sub_j = iota((kh, LANES), 0) // TOK

    def assemble(t):
        for m in range(nz // 2):
            p0 = kall[2 * m, chunk(t)].reshape(kh, LANES)
            p1 = kall[2 * m + 1, chunk(t)].reshape(kh, LANES)
            cols = slice(m * LANES, (m + 1) * LANES)
            kaug[t * kc : t * kc + kh, cols] = cat(p0[:, :HALF], p1[:, :HALF])
            kaug[t * kc + kh : (t + 1) * kc, cols] = cat(p0[:, HALF:], p1[:, HALF:])
        ropes = xin[chunk(t), TOK:, :].reshape(kh, LANES).astype(F32)
        cols = slice(latent, latent + LANES)
        for c in range(2):
            flags = jnp.where(lane_k - HALF == sub_j + (c * ns + t * jc), -BIG, 0.0)
            part = ropes if c == 0 else cat(ropes[:, HALF:], ropes[:, :HALF])
            ext = jnp.where(lane_k < HALF, part, flags).astype(BF16)
            kaug[t * kc + c * kh : t * kc + (c + 1) * kh, cols] = ext

    c2 = SCALE * LOG2E

    def rowsof(b):
        return pl.ds(pl.multiple_of(b * rb, rb), rb)

    def scores(t, lo_b, hi_b):
        @pl.loop(lo_b, hi_b, unroll=nrb // 2)
        def _(b):
            keys = kaug[t * kc : (t + 1) * kc, :]
            raw = dot(keys, qaug[b], 1, 1)
            dprob = dot(keys[:, :latent], qdo[b, rb:, :], 1, 1)
            peak = jnp.max(raw, axis=0, keepdims=True)
            e = jnp.exp2((raw - peak) * c2)
            stat[b, t : t + 1, :] = peak
            stat[b, nt + t : nt + t + 1, :] = jnp.sum(e, axis=0, keepdims=True)
            stat[b, 2 * nt + t : 2 * nt + t + 1, :] = jnp.sum(e * dprob, axis=0, keepdims=True)
            ebuf[t, b] = e
            dpbuf[t, b] = dprob

    half = nrb // 2
    steps = [(("scores", t, n), T_SCORE, t) for t in range(nt) for n in range(2)]
    opens = {t: ARRIVE * (t + 1) for t in range(nt)}
    started = False
    for item in plan(nt, nr, steps, opens, True):
        if item[0] == "event":
            ag_event(*item[1:])
        elif item[0] == "whole":
            assemble(item[1])
        else:
            if not started:
                for copy in in_copies:
                    copy.wait()
                started = True
            scores(item[2], item[3] * half, (item[3] + 1) * half)

    @pl.loop(0, nrb)
    def _(b):
        tops = stat[b, 0:nt, :]
        peak = jnp.max(tops, axis=0, keepdims=True)
        alpha = jnp.exp2((tops - peak) * c2)
        total = jnp.sum(alpha * stat[b, nt : 2 * nt, :], axis=0, keepdims=True)
        inv = 1.0 / total
        fin[b, 0:nt, :] = alpha * inv
        fin[b, nt : nt + 1, :] = (
            jnp.sum(alpha * stat[b, 2 * nt : 3 * nt, :], axis=0, keepdims=True) * inv
        )

    def grads(t, lo_b, hi_b):
        if lo_b == 0:
            acc[...] = jnp.zeros_like(acc)

        @pl.loop(lo_b, hi_b, unroll=nrb // 2)
        def _(b):
            p = ebuf[t, b] * fin[b, t : t + 1, :]
            ds = (p * (dpbuf[t, b] - fin[b, nt : nt + 1, :])) * SCALE
            dsb = ds.astype(BF16)
            dst[b, t * kc : (t + 1) * kc, :] = dsb
            acc[:, :latent] += dot(cat(dsb, p.astype(BF16)), qdo[b])
            acc[:, latent:] += dot(dsb, qaug[b, :, latent:])

    def pieces(t):
        for m in range(nz // 2):
            cols = slice(m * LANES, (m + 1) * LANES)
            a, b = acc[:kh, cols], acc[kh:, cols]
            pf[t, 2 * m, :kh] = cat(a[:, :HALF], b[:, :HALF])
            pf[t, 2 * m + 1, :kh] = cat(a[:, HALF:], b[:, HALF:])
        cols = slice(latent, latent + LANES)
        prs[...] = cat(acc[:kh, cols][:, :HALF], acc[kh:, cols][:, :HALF])
        for zz in range(nz):
            for ii in range(ii_n):
                pf[t, zz, kh + ii * jc : kh + (ii + 1) * jc] = prs[
                    pl.ds(ii_n * zz + ii, jc, stride=TOK), :
                ]

    def rs_copy(t, d, r):
        return pltpu.make_async_remote_copy(
            src_ref=rs_out.at[t, d, r - 1], dst_ref=rs_in.at[t, d, r - 1],
            send_sem=rs_s.at[t, d, r - 1], recv_sem=rs_r.at[t, d, r - 1],
            device_id=(s, right if d == 0 else left), device_id_type=MESH,
        )

    def rs_event(t, d, r):
        n = hops(t, d)
        if r > n:
            return
        away = n + 1 - r
        target = lax.rem(z + away, nz) if d == 0 else lax.rem(z + nz - away, nz)
        val = pf[t, target]
        if r > 1:
            rs_copy(t, d, r - 1).wait_recv()
            val = val + rs_in[t, d, r - 2].astype(F32)
        rs_out[t, d, r - 1] = val.astype(BF16)
        rs_copy(t, d, r).start()

    def rs_final(t):
        val = pf[t, z]
        for d in range(2):
            n = hops(t, d)
            rs_copy(t, d, n).wait_recv()
            val = val + rs_in[t, d, n - 1].astype(F32)
        base_row = t * jc * 2 * TOK
        for j in range(jc):
            yf[base_row + j * 2 * TOK : base_row + j * 2 * TOK + TOK, :] = val[j * TOK : (j + 1) * TOK]
        for ii in range(ii_n):
            yf[pl.ds(base_row + TOK + ii, jc, stride=2 * TOK), :] = val[kh + ii * jc : kh + (ii + 1) * jc]
        block = yf[base_row : base_row + jc * 2 * TOK, :]
        ys[chunk(t)] = block.astype(BF16).reshape(jc, 2 * TOK, LANES)
        first = 0
        if t == 0:
            yin[0] = ys[0]
            first = 1

        @pl.loop(t * jc + first, (t + 1) * jc)
        def _(j):
            pltpu.make_async_remote_copy(
                src_ref=ys.at[j], dst_ref=yin.at[j], send_sem=send_sem.at[2], recv_sem=y_sem,
                device_id=(lax.rem(s + ns - j, ns), z), device_id_type=MESH,
            ).start()

    def dq_copy(b):
        return pltpu.make_async_copy(dqst.at[b], dq_hbm.at[pl.ds(b * rb, rb)], out_sem.at[b])

    def dquery(lo_b, hi_b):
        @pl.loop(lo_b, hi_b)
        def _(b):
            out = dot(dst[b], kaug[...], 0, 0)
            dqst[b] = out[:, :latent].astype(BF16)
            qx[rowsof(b), :] = out[:, latent:]

        for b in range(lo_b, hi_b):
            dq_copy(b).start()

    steps = [(("grads", t, n), T_GRAD, None) for t in range(nt) for n in range(2)]
    steps += [(("dquery", b), T_DQ, None) for b in range(nrb)]
    opens = {t: ("grads", t, 1) for t in range(nt)}
    for item in plan(nt, nr, steps, opens, False):
        if item[0] == "event":
            rs_event(*item[1:])
        elif item[0] == "whole":
            rs_final(item[1])
        elif item[1] == "grads":
            grads(item[2], item[3] * half, (item[3] + 1) * half)
            if item[3] == 1:
                pieces(item[2])
        else:
            dquery(item[2], item[2] + 1)

    for h in range(0, heads, 2):
        a = qx[pl.ds(h, qd, stride=heads), :]
        b = qx[pl.ds(h + 1, qd, stride=heads), :]
        dqr_out[:, h * HALF : (h + 2) * HALF] = cat(a[:, :HALF], b[:, :HALF]).astype(BF16)
    pltpu.make_async_copy(yin.at[pl.ds(1, ns - 1)], yin.at[pl.ds(1, ns - 1)], y_sem).wait()

    for n, (buf, count) in enumerate(((req, ns), (xs, ns), (ys, ns))):
        part = buf.at[pl.ds(1, count - 1)]
        pltpu.make_async_copy(part, part, send_sem.at[n]).wait()
    for t in range(nt):
        for d in range(2):
            for r in range(1, hops(t, d) + 1):
                ag_copy(t, d, r).wait_send()
                rs_copy(t, d, r).wait_send()
    for b in range(nrb):
        dq_copy(b).wait()


def finish(ns, ii_n, dq_in, dqr_in, yin_in, gsc, dq_out, dqr_out, dkl_out, dkr_out, dqv, dqrv, yin, yf, sem, out):
    parts = 4
    step = dq_in.shape[0] // parts
    moves = [(yin_in, yin, None), (dqr_in, dqrv, dqr_out)]
    for n in range(parts):
        rows = pl.ds(n * step, step)
        moves.append((dq_in.at[rows], dqv.at[rows], dq_out.at[rows]))
    loads = [pltpu.make_async_copy(a, b, sem.at[n]) for n, (a, b, _) in enumerate(moves)]
    stores = [pltpu.make_async_copy(b, c, out.at[n]) for n, (_, b, c) in enumerate(moves) if n]
    for copy in loads:
        copy.start()
    for load, store in zip(loads[1:], stores):
        load.wait()
        store.start()
    loads[0].wait()

    yf[...] = yin[...].astype(F32).reshape(yf.shape)

    def tokens(first, n):
        tops, lows = [], []
        for i in range(first, first + n, 2):
            a = yf[pl.ds(i, ns, stride=2 * TOK), :]
            b = yf[pl.ds(i + 1, ns, stride=2 * TOK), :]
            tops.append(cat(a[:, :HALF], b[:, :HALF]))
            lows.append(cat(a[:, HALF:], b[:, HALF:]))
        return jnp.concatenate([cat(*tops), cat(*lows)], axis=0).astype(BF16)

    dkl_out[...] = dot(tokens(0, TOK), gsc[...], 0, 0).astype(BF16)
    dkr_out[...] = dot(gsc[...], tokens(TOK, ii_n), 0, 0).astype(BF16)
    for copy in stores:
        copy.wait()


def local(q_latent, q_rope, kv_latent, kv_rope, grad_out, block_slot, pool, selected):
    ns = lax.axis_size("ctx")
    nz = lax.axis_size("head")
    owned = kv_latent.shape[0]
    qd, heads, latent = q_latent.shape
    rows = qd * heads
    nt = min(NT_MAX, ns // 2)
    rb = min(256, rows // 2)
    nrb = rows // rb
    jc = ns // nt
    kh = jc * TOK
    kc = 2 * kh
    nr = nz // 2
    wide = latent + LANES
    piece = kh + (TOK // nz) * jc
    vmem = pl.BlockSpec(memory_space=pltpu.VMEM)
    hbm = pl.BlockSpec(memory_space=pl.ANY)
    dma = pltpu.SemaphoreType.DMA
    raw = pl.pallas_call(
        functools.partial(kernel, ns, nz, nt, nrb, rb),
        out_shape=(
            jax.ShapeDtypeStruct((rows, latent), BF16),
            jax.ShapeDtypeStruct((qd, heads * HALF), BF16),
            jax.ShapeDtypeStruct((ns, 2 * TOK, LANES), BF16),
            jax.ShapeDtypeStruct((2 * ns, owned), BF16),
        ),
        in_specs=[vmem] * 6 + [hbm] * 2,
        out_specs=(hbm, vmem, vmem, vmem),
        scratch_shapes=[
            pltpu.VMEM((ns, 1, LANES), F32),
            pltpu.VMEM((1, LANES), F32),
            pltpu.VMEM((rows, LANES), F32),
            pltpu.VMEM((ns * 2 * TOK, LANES), F32),
            pltpu.VMEM((ns, 2 * TOK, LANES), BF16),
            pltpu.VMEM((ns, 2 * TOK, LANES), BF16),
            pltpu.VMEM((nz, ns, TOK, LANES), BF16),
            pltpu.VMEM((nt * kc, wide), BF16),
            pltpu.VMEM((nrb, rb, wide), BF16),
            pltpu.VMEM((nrb, 2 * rb, latent), BF16),
            pltpu.VMEM((nt, nrb, kc, rb), F32),
            pltpu.VMEM((nt, nrb, kc, rb), F32),
            pltpu.VMEM((nrb, 16, rb), F32),
            pltpu.VMEM((nrb, 8, rb), F32),
            pltpu.VMEM((nrb, nt * kc, rb), BF16),
            pltpu.VMEM((kc, wide), F32),
            pltpu.VMEM((kh, LANES), F32),
            pltpu.VMEM((nt, nz, piece, LANES), F32),
            pltpu.VMEM((nt, 2, nr, piece, LANES), BF16),
            pltpu.VMEM((nt, 2, nr, piece, LANES), BF16),
            pltpu.VMEM((ns * 2 * TOK, LANES), F32),
            pltpu.VMEM((ns, 2 * TOK, LANES), BF16),
            pltpu.VMEM((nrb, rb, latent), BF16),
            dma,
            dma((nt,)),
            dma,
            dma((3,)),
            dma((nt, 2, nr)),
            dma((nt, 2, nr)),
            dma((nt, 2, nr)),
            dma((nt, 2, nr)),
            dma((3,)),
            dma((nrb,)),
        ],
        compiler_params=pltpu.CompilerParams(
            collective_id=0, has_side_effects=True, vmem_limit_bytes=56 * 1024 * 1024
        ),
        cost_estimate=pl.CostEstimate(
            flops=12 * 10**9, bytes_accessed=8 * 10**6, transcendentals=2 * 10**6
        ),
        name="latent_attention_backward",
    )(
        pool[0].T,
        block_slot.reshape(-1, LANES),
        selected.T,
        q_rope,
        kv_latent.transpose(1, 2, 0).reshape(TOK * HALF, owned),
        kv_rope,
        q_latent.reshape(nrb, rb, latent),
        grad_out.reshape(nrb, rb, latent),
    )
    dq, dqr, dkl, dkr = pl.pallas_call(
        functools.partial(finish, ns, TOK // nz),
        out_shape=(
            jax.ShapeDtypeStruct((rows, latent), BF16),
            jax.ShapeDtypeStruct((qd, heads * HALF), BF16),
            jax.ShapeDtypeStruct((TOK * HALF, owned), BF16),
            jax.ShapeDtypeStruct((owned, TOK * HALF // nz), BF16),
        ),
        in_specs=[hbm, hbm, hbm, vmem],
        out_specs=(hbm, hbm, vmem, vmem),
        scratch_shapes=[
            pltpu.VMEM((rows, latent), BF16),
            pltpu.VMEM((qd, heads * HALF), BF16),
            pltpu.VMEM((ns, 2 * TOK, LANES), BF16),
            pltpu.VMEM((ns * 2 * TOK, LANES), F32),
            dma((6,)),
            dma((6,)),
        ],
        compiler_params=pltpu.CompilerParams(vmem_limit_bytes=60 * 1024 * 1024),
        cost_estimate=pl.CostEstimate(flops=2 * 10**7, bytes_accessed=5 * 10**6, transcendentals=0),
        name="gradient_output",
    )(*raw)
    return (
        dq.reshape(qd, heads, latent),
        dqr,
        dkl.reshape(TOK, HALF, owned).transpose(2, 0, 1),
        dkr,
    )


def solution(mesh):
    return jax.shard_map(
        local,
        mesh=mesh,
        in_specs=(
            P("ctx", "head", None),
            P("ctx", "head"),
            P("ctx", None, "head"),
            P("ctx", None),
            P("ctx", "head", None),
            P(),
            P("ctx", None, None),
            P("ctx", None),
        ),
        out_specs=(
            P("ctx", "head", None),
            P("ctx", "head"),
            P("ctx", None, "head"),
            P("ctx", "head"),
        ),
        check_vma=False,
    )
```

time: 348 us -> 76.2 us (0.22)
  matrix products: 128 us -> 0 us
  waiting for transfers between devices: 99.3 us -> 0 us
  Pallas kernels: 0 us -> 75.2 us
  local copies, waits for them, and re-layouts: 35.1 us -> 0 us
  blocking collectives: 27.7 us -> 0 us
  other arithmetic: 23.6 us -> 0 us
  starting transfers between devices: 19.4 us -> 0 us
  between operations: 13.9 us -> 0.8 us
    dot_general x16 -> x0, matrix products: 128 us -> none  [the longest x2 28.9 us: one_block(): jnp.einsum('qhk,qhl->kl', dscores, q_lat, preferred_element_type=jnp.floa...]
    pallas_call x0 -> x2, Pallas kernels: none -> 75.2 us  [the longest x1 71.2 us: local(): pl.pallas_call(functools.partial(kernel, ns, nz, nt, nrb, rb), out_shape=...]
    reduce_scatter x2 -> x0, waiting for transfers between devices: 48.3 us -> none  [the longest x1 48.3 us: local(): lax.psum_scatter(summed_latent, 'head', scatter_dimension=2, tiled=True)]
    all_to_all x3 -> x0, waiting for transfers between devices: 31.9 us -> none  [the longest x1 24.4 us: local(): lax.all_to_all(grad_latent, 'ctx', split_axis=0, concat_axis=0, tiled=True)]
    all_to_all x2 -> x0, blocking collectives: 27.7 us -> none  [the longest x1 15.3 us: local(): lax.all_to_all(local_rows, 'ctx', split_axis=0, concat_axis=0, tiled=True)]
    all_to_all x3 -> x0, starting transfers between devices: 19.3 us -> none  [the longest x1 11.2 us: local(): lax.all_to_all(full_latent[requests], 'ctx', split_axis=0, concat_axis=0,...]
    all_gather x1 -> x0, waiting for transfers between devices: 19.2 us -> none  [local(): full_latent = lax.all_gather(kv_latent, 'head', axis=2, tiled=True)]
    scatter-add x2 -> x0, other arithmetic: 11 us -> none  [the longest x1 9.07 us: local(): summed_latent = jnp.zeros((owned, block_len, width), jnp.float32).at[flat...]
  transfers between devices with their start and end apart: 6 -> 0, of which waited for: 4 -> 0; matrix products, arithmetic and copies ran while one was open for 13% -> 0% of each run, Pallas kernels for 0% -> 0%
where the time goes in v1:
time: 76.2 us; the launch traced here: 76 us
  Pallas kernels  75.2 us (99%)
  between operations  0.8 us (1%)
    pallas_call x1, Pallas kernels, local(): pl.pallas_call(functools.partial(kernel, ns, nz, nt, nrb, rb), out_shape=...  71.2 us
    pallas_call x1, Pallas kernels, local(): pl.pallas_call(functools.partial(finish, ns, TOK // nz), out_shape=(jax.S...  4.04 us

profile of v1, /device:TPU:1, one launch (start us, length us, event | category | flops | bytes accessed | tf_op | source)
XLA Modules:
  0.0 76.0 jit_solution(2072662244899959605)
XLA Ops:
  0.6 71.2 %latent_attention_backward.1 = (bf16[2048,512]{1,0:T(8,128)(2,1)}, bf16[128,1024]{1,0:T(8,128)(2,1)}, bf16[32,32,128]{2,1,0:T(8,128)(2,1)}, bf16[64,128]{1,0:T(8,128)(2,1)}) custom-call(s32[2,32]{1,0:T(2,128)} %bitcast.21, s32[32,128]{1,0:T(8,128)} %bitcast.19, s32[32,128]{1,0:T(8,128)} %bitcast.20, bf16[128,1024]{1,0:T(8,128)(2,1)} %qrope_ref.1, ...), custom_call_target="tpu_custom_call" | custom-call | flops 12000000000 | bytes 8000000 | tf_op jit(solution)/shard_map/latent_attention_backward/pallas_call | solution.py:450
  71.8 4.0 %gradient_output.1 = (bf16[2048,512]{1,0:T(8,128)(2,1)}, bf16[128,1024]{1,0:T(8,128)(2,1)}, bf16[1024,128]{1,0:T(8,128)(2,1)}, bf16[128,128]{1,0:T(8,128)(2,1)}) custom-call(bf16[2048,512]{1,0:T(8,128)(2,1)} %get-tuple-element.12.dq_in, bf16[128,1024]{1,0:T(8,128)(2,1)} %get-tuple-element.13.dqr_in, bf16[32,32,128]{2,1,0:T(8,128)(2,1)} %get-tuple-element.14.yin_in, ...), custom_call_target="tpu_custom_call" | custom-call | flops 20000000 | bytes 5000000 | tf_op jit(solution)/shard_map/gradient_output/pallas_call | solution.py:512

commit v2 on v1

--- a/solution.py
+++ b/solution.py
@@ -17,7 +17,7 @@
 HALF = 64
 LANES = 128
 NT_MAX = 4
-PIECE, DELAY, ARRIVE = 0.85, 1.5, 1.0
+PIECE, DELAY, ARRIVE, T_SEND = 0.85, 1.5, 2.0, 0.7
 T_SCORE, T_GRAD, T_DQ, T_EVENT = 0.9, 0.75, 0.55, 0.1
 
 
@@ -25,9 +25,9 @@
     return nr if (t + d) % 2 == 0 else nr - 1
 
 
-def plan(nt, nr, steps, opens, needs):
+def plan(nt, nr, steps, opens):
     order, free, now, left = [], [0.0, 0.0], 0.0, {t: 2 for t in range(nt)}
-    ready = [(at, t, d, 1) for t, at in opens.items() if not isinstance(at, tuple) for d in range(2)]
+    ready = []
     whole = {}
     steps = list(steps)
     while steps or ready:
@@ -47,13 +47,13 @@
                     order.append(("whole", t))
                     whole[t] = now
             continue
-        if steps and (not needs or steps[0][2] in whole):
+        if steps and (steps[0][2] is None or steps[0][2] in whole):
             name, took, _ = steps.pop(0)
             order.append(("step",) + name)
             now += took
             for t, at in opens.items():
-                if at == name:
-                    ready += [(now, t, d, 1) for d in range(2)]
+                if at[0] == name:
+                    ready += [(now + at[1], t, d, 1) for d in range(2)]
             continue
         now = min(e[0] for e in ready)
     return order
@@ -73,9 +73,9 @@
 
 def kernel(
     ns, nz, nt, nrb, rb,
-    pool_ref, slot_ref, sel_ref, qrope_ref, kvl_ref, kvr_ref, q_hbm, do_hbm,
+    pool_hbm, slot_hbm, sel_hbm, qrope_hbm, kvl_hbm, kvr_hbm, q_hbm, do_hbm,
     dq_hbm, dqr_out, yin, gsc,
-    req, reqs, qx, xf, xs, xin, kall, kaug, qaug, qdo, ebuf, dpbuf, stat, fin, dst, acc,
+    pool_ref, slot_ref, sel_ref, qrope_ref, kvl_ref, kvr_ref, req, reqs, qx, xf, xs, xin, kall, kaug, qaug, qdo, ebuf, dpbuf, stat, fin, dst, acc,
     prs, pf, rs_out, rs_in, yf, ys, dqst,
     req_sem, x_sem, y_sem, send_sem, ag_s, ag_r, rs_s, rs_r, in_sem, out_sem,
 ):
@@ -90,8 +90,12 @@
     owned = kvl_ref.shape[1]
     qd = sel_ref.shape[1]
     heads = (nrb * rb) // qd
-    right = lax.rem(z + 1, nz)
-    left = lax.rem(z + nz - 1, nz)
+
+    def wrap(i, n):
+        return jnp.where(i >= n, i - n, i)
+
+    right = wrap(z + 1, nz)
+    left = wrap(z + nz - 1, nz)
 
     def hops(t, d):
         return hops_of(nr, t, d)
@@ -100,7 +104,7 @@
 
     @pl.loop(1, ns)
     def _(j):
-        pl.semaphore_signal(barrier, inc=1, device_id=(lax.rem(s + j, ns), z), device_id_type=MESH)
+        pl.semaphore_signal(barrier, inc=1, device_id=(wrap(s + j, ns), z), device_id_type=MESH)
 
     for zn in (left, right):
         pl.semaphore_signal(barrier, inc=1, device_id=(s, zn), device_id_type=MESH)
@@ -110,8 +114,19 @@
         pltpu.make_async_copy(do_hbm, qdo.at[:, pl.ds(rb, rb)], in_sem.at[1]),
         pltpu.make_async_copy(q_hbm, qdo.at[:, pl.ds(0, rb)], in_sem.at[2]),
     ]
-    for copy in in_copies:
+    small = [
+        pltpu.make_async_copy(a, b, in_sem.at[3 + n])
+        for n, (a, b) in enumerate(
+            (
+                (pool_hbm, pool_ref), (slot_hbm, slot_ref), (sel_hbm, sel_ref),
+                (qrope_hbm, qrope_ref), (kvl_hbm, kvl_ref), (kvr_hbm, kvr_ref),
+            )
+        )
+    ]
+    for copy in small + in_copies:
         copy.start()
+    small[0].wait()
+    small[1].wait()
 
     pools = pool_ref[...].astype(F32)
     wanted = cat(pools[0:1], pools[1:2], jnp.full((1, LANES - 2 * ns), -1.0, F32))
@@ -141,10 +156,12 @@
     def _(j):
         pltpu.make_async_remote_copy(
             src_ref=reqs, dst_ref=req.at[j], send_sem=send_sem.at[0], recv_sem=req_sem,
-            device_id=(lax.rem(s + ns - j, ns), z), device_id_type=MESH,
+            device_id=(wrap(s + ns - j, ns), z), device_id_type=MESH,
         ).start()
 
     yf[...] = jnp.zeros_like(yf)
+    small[2].wait()
+    small[3].wait()
     places = iota((HALF, 1), 0)
     cpos = places // ns
     slotv = 2 * lax.rem(s + 2 * ns - (places - cpos * ns), ns) + cpos
@@ -170,6 +187,8 @@
         picks.append((iota((ns, owned), 1).astype(F32) == mine).astype(F32))
     gsc[...] = jnp.concatenate(picks, axis=0).astype(BF16)
     g = gsc[...]
+    small[4].wait()
+    small[5].wait()
     lat = dot(g, kvl_ref[...], 1, 1)
     rop = dot(g, kvr_ref[...])
     for i in range(TOK):
@@ -179,18 +198,19 @@
     xs[...] = xf[...].astype(BF16).reshape(xs.shape)
     xin[0] = xs[0]
 
-    @pl.loop(1, ns)
-    def _(j):
-        pltpu.make_async_remote_copy(
-            src_ref=xs.at[j], dst_ref=xin.at[j], send_sem=send_sem.at[1], recv_sem=x_sem.at[j // jc],
-            device_id=(lax.rem(s + j, ns), z), device_id_type=MESH,
-        ).start()
+    def xsend(t):
+        @pl.loop(max(1, t * jc), (t + 1) * jc)
+        def _(j):
+            pltpu.make_async_remote_copy(
+                src_ref=xs.at[j], dst_ref=xin.at[j], send_sem=send_sem.at[1], recv_sem=x_sem.at[t],
+                device_id=(wrap(s + j, ns), z), device_id_type=MESH,
+            ).start()
 
     def chunk(t):
         return pl.ds(t * jc, jc)
 
     def ag_copy(t, d, r):
-        zs = lax.rem(z + nz - (r - 1), nz) if d == 0 else lax.rem(z + (r - 1), nz)
+        zs = wrap(z + nz - (r - 1), nz) if d == 0 else wrap(z + (r - 1), nz)
         piece = kall.at[zs, chunk(t)]
         return pltpu.make_async_remote_copy(
             src_ref=piece, dst_ref=piece, send_sem=ag_s.at[t, d, r - 1], recv_sem=ag_r.at[t, d, r - 1],
@@ -198,7 +218,7 @@
         )
 
     def ag_wait(t, d, r):
-        zs = lax.rem(z + nz - r, nz) if d == 0 else lax.rem(z + r, nz)
+        zs = wrap(z + nz - r, nz) if d == 0 else wrap(z + r, nz)
         piece = kall.at[zs, chunk(t)]
         pltpu.make_async_copy(piece, piece, ag_r.at[t, d, r - 1]).wait()
 
@@ -251,14 +271,17 @@
             dpbuf[t, b] = dprob
 
     half = nrb // 2
-    steps = [(("scores", t, n), T_SCORE, t) for t in range(nt) for n in range(2)]
-    opens = {t: ARRIVE * (t + 1) for t in range(nt)}
+    steps = [(("xsend", t), T_SEND, None) for t in range(nt)]
+    steps += [(("scores", t, n), T_SCORE, t) for t in range(nt) for n in range(2)]
+    opens = {t: (("xsend", t), ARRIVE) for t in range(nt)}
     started = False
-    for item in plan(nt, nr, steps, opens, True):
+    for item in plan(nt, nr, steps, opens):
         if item[0] == "event":
             ag_event(*item[1:])
         elif item[0] == "whole":
             assemble(item[1])
+        elif item[1] == "xsend":
+            xsend(item[2])
         else:
             if not started:
                 for copy in in_copies:
@@ -317,7 +340,7 @@
         if r > n:
             return
         away = n + 1 - r
-        target = lax.rem(z + away, nz) if d == 0 else lax.rem(z + nz - away, nz)
+        target = wrap(z + away, nz) if d == 0 else wrap(z + nz - away, nz)
         val = pf[t, target]
         if r > 1:
             rs_copy(t, d, r - 1).wait_recv()
@@ -347,7 +370,7 @@
         def _(j):
             pltpu.make_async_remote_copy(
                 src_ref=ys.at[j], dst_ref=yin.at[j], send_sem=send_sem.at[2], recv_sem=y_sem,
-                device_id=(lax.rem(s + ns - j, ns), z), device_id_type=MESH,
+                device_id=(wrap(s + ns - j, ns), z), device_id_type=MESH,
             ).start()
 
     def dq_copy(b):
@@ -365,8 +388,8 @@
 
     steps = [(("grads", t, n), T_GRAD, None) for t in range(nt) for n in range(2)]
     steps += [(("dquery", b), T_DQ, None) for b in range(nrb)]
-    opens = {t: ("grads", t, 1) for t in range(nt)}
-    for item in plan(nt, nr, steps, opens, False):
+    opens = {t: (("grads", t, 1), 0.0) for t in range(nt)}
+    for item in plan(nt, nr, steps, opens):
         if item[0] == "event":
             rs_event(*item[1:])
         elif item[0] == "whole":
@@ -382,11 +405,6 @@
         a = qx[pl.ds(h, qd, stride=heads), :]
         b = qx[pl.ds(h + 1, qd, stride=heads), :]
         dqr_out[:, h * HALF : (h + 2) * HALF] = cat(a[:, :HALF], b[:, :HALF]).astype(BF16)
-    pltpu.make_async_copy(yin.at[pl.ds(1, ns - 1)], yin.at[pl.ds(1, ns - 1)], y_sem).wait()
-
-    for n, (buf, count) in enumerate(((req, ns), (xs, ns), (ys, ns))):
-        part = buf.at[pl.ds(1, count - 1)]
-        pltpu.make_async_copy(part, part, send_sem.at[n]).wait()
     for t in range(nt):
         for d in range(2):
             for r in range(1, hops(t, d) + 1):
@@ -394,6 +412,10 @@
                 rs_copy(t, d, r).wait_send()
     for b in range(nrb):
         dq_copy(b).wait()
+    for n, buf in enumerate((req, xs, ys)):
+        part = buf.at[pl.ds(1, ns - 1)]
+        pltpu.make_async_copy(part, part, send_sem.at[n]).wait()
+    pltpu.make_async_copy(yin.at[pl.ds(1, ns - 1)], yin.at[pl.ds(1, ns - 1)], y_sem).wait()
 
 
 def finish(ns, ii_n, dq_in, dqr_in, yin_in, gsc, dq_out, dqr_out, dkl_out, dkr_out, dqv, dqrv, yin, yf, sem, out):
@@ -455,9 +477,15 @@
             jax.ShapeDtypeStruct((ns, 2 * TOK, LANES), BF16),
             jax.ShapeDtypeStruct((2 * ns, owned), BF16),
         ),
-        in_specs=[vmem] * 6 + [hbm] * 2,
+        in_specs=[hbm] * 8,
         out_specs=(hbm, vmem, vmem, vmem),
         scratch_shapes=[
+            pltpu.VMEM((2, ns), jnp.int32),
+            pltpu.VMEM((block_slot.shape[0] // LANES, LANES), jnp.int32),
+            pltpu.VMEM((selected.shape[1], qd), jnp.int32),
+            pltpu.VMEM((qd, heads * HALF), BF16),
+            pltpu.VMEM((TOK * HALF, owned), BF16),
+            pltpu.VMEM((owned, TOK * HALF), BF16),
             pltpu.VMEM((ns, 1, LANES), F32),
             pltpu.VMEM((1, LANES), F32),
             pltpu.VMEM((rows, LANES), F32),
@@ -489,7 +517,7 @@
             dma((nt, 2, nr)),
             dma((nt, 2, nr)),
             dma((nt, 2, nr)),
-            dma((3,)),
+            dma((9,)),
             dma((nrb,)),
         ],
         compiler_params=pltpu.CompilerParams(

time: 76.2 us -> 74.5 us (0.978)
  Pallas kernels: 75.2 us -> 73.5 us
    pallas_call x1, Pallas kernels: 71.2 us -> 69.5 us  [local(): pl.pallas_call(functools.partial(kernel, ns, nz, nt, nrb, rb), out_shape=...]
where the time goes in v2:
time: 74.5 us; the launch traced here: 74.3 us
  Pallas kernels  73.5 us (99%)
  between operations  0.8 us (1%)
    pallas_call x1, Pallas kernels, local(): pl.pallas_call(functools.partial(kernel, ns, nz, nt, nrb, rb), out_shape=...  69.5 us
    pallas_call x1, Pallas kernels, local(): pl.pallas_call(functools.partial(finish, ns, TOK // nz), out_shape=(jax.S...  4.04 us

profile of v2, /device:TPU:1, one launch (start us, length us, event | category | flops | bytes accessed | tf_op | source)
XLA Modules:
  0.0 74.3 jit_solution(698234416624443698)
XLA Ops:
  0.6 69.5 %latent_attention_backward.1 = (bf16[2048,512]{1,0:T(8,128)(2,1)}, bf16[128,1024]{1,0:T(8,128)(2,1)}, bf16[32,32,128]{2,1,0:T(8,128)(2,1)}, bf16[64,128]{1,0:T(8,128)(2,1)}) custom-call(s32[2,32]{1,0:T(2,128)} %bitcast.21, s32[32,128]{1,0:T(8,128)} %bitcast.19, s32[32,128]{1,0:T(8,128)} %bitcast.20, bf16[128,1024]{1,0:T(8,128)(2,1)} %qrope_hbm.1, ...), custom_call_target="tpu_custom_call" | custom-call | flops 12000000000 | bytes 8000000 | tf_op jit(solution)/shard_map/latent_attention_backward/pallas_call | solution.py:472
  70.1 4.0 %gradient_output.1 = (bf16[2048,512]{1,0:T(8,128)(2,1)}, bf16[128,1024]{1,0:T(8,128)(2,1)}, bf16[1024,128]{1,0:T(8,128)(2,1)}, bf16[128,128]{1,0:T(8,128)(2,1)}) custom-call(bf16[2048,512]{1,0:T(8,128)(2,1)} %get-tuple-element.12.dq_in, bf16[128,1024]{1,0:T(8,128)(2,1)} %get-tuple-element.13.dqr_in, bf16[32,32,128]{2,1,0:T(8,128)(2,1)} %get-tuple-element.14.yin_in, ...), custom_call_target="tpu_custom_call" | custom-call | flops 20000000 | bytes 5000000 | tf_op jit(solution)/shard_map/gradient_output/pallas_call | solution.py:540

commit v3 on v2

--- a/solution.py
+++ b/solution.py
@@ -419,7 +419,7 @@
 
 
 def finish(ns, ii_n, dq_in, dqr_in, yin_in, gsc, dq_out, dqr_out, dkl_out, dkr_out, dqv, dqrv, yin, yf, sem, out):
-    parts = 4
+    parts = 16
     step = dq_in.shape[0] // parts
     moves = [(yin_in, yin, None), (dqr_in, dqrv, dqr_out)]
     for n in range(parts):
@@ -552,8 +552,8 @@
             pltpu.VMEM((qd, heads * HALF), BF16),
             pltpu.VMEM((ns, 2 * TOK, LANES), BF16),
             pltpu.VMEM((ns * 2 * TOK, LANES), F32),
-            dma((6,)),
-            dma((6,)),
+            dma((18,)),
+            dma((18,)),
         ],
         compiler_params=pltpu.CompilerParams(vmem_limit_bytes=60 * 1024 * 1024),
         cost_estimate=pl.CostEstimate(flops=2 * 10**7, bytes_accessed=5 * 10**6, transcendentals=0),

time: 74.5 us -> 74.7 us (level)
  no operation moved by 1% of the time
where the time goes in v3:
time: 74.7 us; the launch traced here: 74.5 us
  Pallas kernels  73.7 us (99%)
  between operations  0.8 us (1%)
    pallas_call x1, Pallas kernels, local(): pl.pallas_call(functools.partial(kernel, ns, nz, nt, nrb, rb), out_shape=...  69.5 us
    pallas_call x1, Pallas kernels, local(): pl.pallas_call(functools.partial(finish, ns, TOK // nz), out_shape=(jax.S...  4.15 us

profile of v3, /device:TPU:1, one launch (start us, length us, event | category | flops | bytes accessed | tf_op | source)
XLA Modules:
  0.0 74.5 jit_solution(216702762090352395)
XLA Ops:
  0.6 69.5 %latent_attention_backward.1 = (bf16[2048,512]{1,0:T(8,128)(2,1)}, bf16[128,1024]{1,0:T(8,128)(2,1)}, bf16[32,32,128]{2,1,0:T(8,128)(2,1)}, bf16[64,128]{1,0:T(8,128)(2,1)}) custom-call(s32[2,32]{1,0:T(2,128)} %bitcast.21, s32[32,128]{1,0:T(8,128)} %bitcast.19, s32[32,128]{1,0:T(8,128)} %bitcast.20, bf16[128,1024]{1,0:T(8,128)(2,1)} %qrope_hbm.1, ...), custom_call_target="tpu_custom_call" | custom-call | flops 12000000000 | bytes 8000000 | tf_op jit(solution)/shard_map/latent_attention_backward/pallas_call | solution.py:472
  70.1 4.2 %gradient_output.1 = (bf16[2048,512]{1,0:T(8,128)(2,1)}, bf16[128,1024]{1,0:T(8,128)(2,1)}, bf16[1024,128]{1,0:T(8,128)(2,1)}, bf16[128,128]{1,0:T(8,128)(2,1)}) custom-call(bf16[2048,512]{1,0:T(8,128)(2,1)} %get-tuple-element.12.dq_in, bf16[128,1024]{1,0:T(8,128)(2,1)} %get-tuple-element.13.dqr_in, bf16[32,32,128]{2,1,0:T(8,128)(2,1)} %get-tuple-element.14.yin_in, ...), custom_call_target="tpu_custom_call" | custom-call | flops 20000000 | bytes 5000000 | tf_op jit(solution)/shard_map/gradient_output/pallas_call | solution.py:540
